TPU v7x, 32 devices: a whole 2x2x4 slice. The times are simulated.
32 devices in a mesh: blk: 8 (over y, x, core), tm: 4 (over z).
Axes of the slice: x: 2, y: 2, z: 4, core: 2. Of those that a mesh axis runs over, the one named last changes fastest.
Arguments:
- records: bfloat16 [2048, 16, 512], P('blk', 'tm'), may hold values from -6 to 6
- glitch_mask: int32 [2048, 16], P('blk'), may hold values 0 or 1
- fir_taps: bfloat16 [65], replicated, may hold values from -1.1953125 to 1.1953125
Outputs:
- correlations: bfloat16 [16, 2048, 2048], P('tm', 'blk')
All inputs are finite; a program needn't handle non-finite values. No bound on the sum of `glitch_mask` on one device may be relied on, other than what follows from the above.
Results may differ from a plain program's by a relative error of at most 0.015.
Values may be sent and summed in bfloat16 or wider, within the bound.
A program may use at most 256 MiB of HBM per device.

v0:
```python
import math
import jax
import jax.numpy as jnp
import numpy as np
from jax import lax
from jax.sharding import PartitionSpec as P

BINS = 128
FIRST_BIN = 16
SMOOTH = 64
LAGS = 16


def dft_thirds(seglen):
    sample = np.arange(seglen)[:, None]
    freq = np.arange(BINS)[None, :] + FIRST_BIN
    angle = sample * freq % seglen * (2.0 * math.pi / seglen)
    rest = np.concatenate([np.cos(angle), -np.sin(angle)], axis=1).astype(np.float32)
    thirds = []
    for _ in range(3):
        part = rest.astype(jnp.bfloat16)
        thirds.append(part)
        rest = rest - part.astype(np.float32)
    return np.concatenate(thirds, axis=1)


def lag_rows(seg_total, seglen):
    delay = np.arange(LAGS)[:, None] - LAGS // 2
    freq = np.arange(BINS)[None, :] + FIRST_BIN
    angle = delay * freq % seglen * (2.0 * math.pi / seglen)
    factor = 1.0 / math.sqrt(seg_total * BINS)
    tables = np.stack([np.cos(angle), np.sin(angle)]).astype(np.float32) * np.float32(factor)
    return tables.astype(jnp.bfloat16).astype(np.float32)


def filter_matrix(fir_taps, seglen):
    half = (fir_taps.shape[0] - 1) // 2
    period = 2 * seglen
    line = jnp.pad(fir_taps[::-1], (seglen - 1 - half, seglen - half))
    rows = jnp.tile(line, seglen)[: seglen * (period - 1)].reshape(seglen, period - 1)
    return rows[:, seglen - 1 :]


def transform_table(fir_taps, seglen):
    parts = jnp.dot(
        filter_matrix(fir_taps, seglen),
        jnp.asarray(dft_thirds(seglen)),
        preferred_element_type=jnp.float32,
    )
    width = 2 * BINS
    total = parts[:, :width] + (parts[:, width : 2 * width] + parts[:, 2 * width :])
    return total.astype(jnp.bfloat16)


def whiten(samples, usable, fir_taps):
    seglen = samples.shape[1]
    source = lax.broadcasted_iota(jnp.int32, (seglen, seglen), 0)
    target = lax.broadcasted_iota(jnp.int32, (seglen, seglen), 1)
    band_ones = jnp.where(jnp.abs(source - target) <= SMOOTH, 1.0, 0.0).astype(jnp.bfloat16)
    where = lax.broadcasted_iota(jnp.int32, (1, seglen), 1)
    counts = jnp.minimum(where, SMOOTH) + jnp.minimum(seglen - 1 - where, SMOOTH) + 1
    envelope = jnp.dot(
        jnp.abs(samples), band_ones, preferred_element_type=jnp.float32
    ) / counts.astype(jnp.float32)
    normal = (samples.astype(jnp.float32) / (envelope + 1e-06)).astype(jnp.bfloat16)
    spectra = jnp.dot(normal, transform_table(fir_taps, seglen), preferred_element_type=jnp.float32)
    power = jnp.sum(spectra * spectra, axis=1, keepdims=True) * jnp.float32(1.0 / BINS)
    scale = usable.astype(jnp.float32)[:, None] / jnp.sqrt(power + 1e-06)
    return (spectra * scale).astype(jnp.bfloat16)


def body(records, glitch_mask, fir_taps):
    tm_count = lax.axis_size("tm")
    tm_index = lax.axis_index("tm")
    chans, segs, seglen = records.shape
    seg_total = glitch_mask.shape[1]
    usable = lax.dynamic_slice_in_dim(glitch_mask, tm_index * segs, segs, 1)
    white = whiten(records.reshape(chans * segs, seglen), usable.reshape(chans * segs), fir_taps)
    slab = white.reshape(chans, segs * 2 * BINS)
    column = lax.all_gather(slab, "tm", axis=1, tiled=True)
    every = lax.all_gather(column, "blk", axis=0, tiled=True)
    lags_dev = LAGS // tm_count
    tables = lax.dynamic_slice_in_dim(
        jnp.asarray(lag_rows(seg_total, seglen)), tm_index * lags_dev, lags_dev, 1
    )
    cos_rows = tables[0][:, None, None, :]
    sin_rows = tables[1][:, None, None, :]
    own = column.reshape(chans, seg_total, 2, BINS).astype(jnp.float32)
    real_part, imag_part = (own[None, :, :, 0], own[None, :, :, 1])
    turned = jnp.stack(
        [cos_rows * real_part - sin_rows * imag_part, cos_rows * imag_part + sin_rows * real_part],
        axis=3,
    ).astype(jnp.bfloat16)
    left = turned.reshape(lags_dev, chans, seg_total * 2 * BINS)
    return jnp.einsum("lik,jk->lij", left, every, preferred_element_type=jnp.float32).astype(
        jnp.bfloat16
    )


def solution(mesh):
    placed = (P("blk", "tm", None), P("blk", None), P())
    return jax.shard_map(
        body, mesh=mesh, in_specs=placed, out_specs=P("tm", "blk", None), check_vma=False
    )
```

profile of v0, /device:TPU:0, one launch (start us, length us, event | category | flops | bytes accessed | tf_op | source)
XLA Modules:
  0.0 192.0 jit_solution(9935563108440876466)
XLA Ops:
  6.5 0.0 all-gather.3.cloned.1.call-start
  6.5 1.8 abs.10
  8.3 2.4 %reshape.75 = f32[1024,512]{1,0:T(8,128)} reshape(bf16[256,4,512]{2,1,0:T(4,128)(2,1)} %param.5) | data formatting | bytes 3145728 | tf_op jit(solution)/shard_map/convert_element_type | solution.py:65
  10.7 0.7 dynamic-slice_convert_fusion
  11.4 0.1 copy.6
  11.6 0.1 convert_element_type.59
  11.7 0.7 rev.3
  12.5 0.1 pad.4
  12.5 0.2 broadcast_bitcast_fusion
  12.8 0.3 copy.8
  13.1 1.6 reshape.73
  14.7 1.1 abs.11
  15.8 1.7 fusion.11
  17.6 3.1 %multiply_reduce_fusion = (f32[1024]{0:T(1024)S(1)}, f32[1024,256]{0,1:T(8,128)S(1)}) fusion(f32[512,768]{1,0:T(8,128)S(1)} %fusion.11, f32[1024,512]{1,0:T(8,128)} %reshape.75, bf16[1024,512]{1,0:T(8,128)(2,1)} %abs.11, f32[512]{0:T(512)S(1)} %fusion.22), kind=kOutput, calls=%fused_computation.10 | convolution fusion | flops 809630720 | bytes 5773312 | tf_op jit(solution)/shard_map/dot_general | solution.py:66
  20.7 0.1 multiply_convert_fusion
  20.8 0.2 copy.7
  21.0 1.1 reshape.74
  22.1 0.0 all-gather.3.cloned.1.call-update
  22.1 0.2 all-gather.5.cloned.1.call-start
  22.3 48.6 %all-gather.3.cloned.1.call-done = bf16[256,4096]{1,0:T(8,128)(2,1)} async-done(((bf16[256,1024]{1,0:T(8,128)(2,1)}), bf16[256,4096]{1,0:T(8,128)(2,1)}) %all-gather.3.cloned.1.call-update) | async-done | bytes 2097168 | tf_op jit(solution)/shard_map/all_gather | solution.py:80
  70.9 0.0 all-gather.5.cloned.1.call-update
  70.9 0.7 dynamic-slice_bitcast_fusion.1
  71.7 6.6 %reshape.76 = f32[256,16,2,128]{3,2,1,0:T(2,128)} reshape(bf16[256,4096]{1,0:T(8,128)(2,1)} %all-gather.3.cloned.1.call-done) | data formatting | bytes 6291456 | tf_op jit(solution)/shard_map/convert_element_type | solution.py:88
  78.2 10.3 %fusion.31 = (f32[256,16,1,128]{3,2,1,0:T(1,128)S(1)}, f32[256,16,1,128]{3,2,1,0:T(1,128)}) fusion(f32[256,16,2,128]{3,2,1,0:T(2,128)} %reshape.76), kind=kLoop, calls=%fused_computation.38 | loop fusion | bytes 8388608 | tf_op jit(solution)/shard_map/slice | solution.py:89
  88.5 18.6 %subtract_convert_fusion = (bf16[4,256,16,1,128]{4,3,2,1,0:T(2,128)(2,1)S(1)}, bf16[4,256,16,1,128]{4,3,2,1,0:T(2,128)(2,1)S(1)}) fusion(f32[256,16,128]{2,1,0:T(8,128)} %bitcast.27, f32[4,128]{1,0:T(4,128)S(1)} %get-tuple-element.10, f32[256,16,128]{2,1,0:T(8,128)S(1)} %bitcast.26, f32[4,128]{1,0:T(4,128)S(1)} %get-tuple-element.9), kind=kLoop, calls=%fused_computation.4 | loop fusion | flops 16777216 | bytes 12587008 | tf_op jit(solution)/shard_map/convert.2
  107.2 20.3 %pad_maximum_fusion = bf16[4,256,16,2,128]{4,3,2,1,0:T(2,128)(2,1)} fusion(bf16[4,256,16,1,128]{4,3,2,1,0:T(2,128)(2,1)S(1)} %get-tuple-element.6, bf16[4,256,16,1,128]{4,3,2,1,0:T(2,128)(2,1)S(1)} %get-tuple-element.5), kind=kLoop, calls=%fused_computation.2 | loop fusion | flops 16777216 | bytes 16777216 | tf_op jit(solution)/shard_map/stack | solution.py:90
  127.5 14.5 %convert_element_type.63 = bf16[4,256,4096]{2,1,0:T(8,128)(2,1)} reshape(bf16[4,256,16,2,128]{4,3,2,1,0:T(2,128)(2,1)} %pad_maximum_fusion) | data formatting | bytes 16777216 | tf_op jit(solution)/shard_map/convert_element_type | solution.py:93
  142.0 19.4 %all-gather.5.cloned.1.call-done = bf16[2048,4096]{1,0:T(8,128)(2,1)} async-done(((bf16[256,4096]{1,0:T(8,128)(2,1)}), bf16[2048,4096]{1,0:T(8,128)(2,1)}) %all-gather.5.cloned.1.call-update) | async-done | bytes 16777232 | tf_op jit(solution)/shard_map/all_gather | solution.py:81
  161.4 23.8 %fusion.2 = bf16[4,256,2048]{2,1,0:T(8,128)(2,1)} fusion(bf16[4,256,4096]{2,1,0:T(8,128)(2,1)} %convert_element_type.63, bf16[2048,4096]{1,0:T(8,128)(2,1)} %all-gather.5.cloned.1.call-done), kind=kOutput, calls=%fused_computation.5 | convolution fusion | flops 17181966336 | bytes 29360128 | tf_op jit(solution)/shard_map/lik,jk->lij/dot_general | solution.py:95
  (2 shorter events, 0.0 us)
Async XLA Ops:
  6.5 64.4 %all-gather.3.cloned.1.call-start = ((), (), s32[]{:S(2)}) async-start(), calls=%async_computation | async-start | bytes 2621440 | tf_op jit(solution)/shard_map/all_gather | solution.py:80
  22.1 139.3 %all-gather.5.cloned.1.call-start = ((), (), s32[]{:S(2)}) async-start(), calls=%async_computation.1 | async-start | bytes 18874368 | tf_op jit(solution)/shard_map/all_gather | solution.py:81
Sparse Core Ops, SparseCore 0:
  22.2 48.6 all-gather.2
  72.8 88.5 all-gather.4
where the time goes:
time: 193 us; the launch traced here: 192 us
  waiting for transfers between devices  68 us (35%)
  other arithmetic  41.5 us (22%)
  local copies, waits for them, and re-layouts  40.2 us (21%)
  matrix products  28.6 us (15%)
  between operations  13.5 us (7%)
    all_gather x1, waiting for transfers between devices, body(): column = lax.all_gather(slab, 'tm', axis=1, tiled=True)  48.6 us
    dot_general x1, matrix products, body(): jnp.einsum('lik,jk->lij', left, every, preferred_element_type=jnp.float32)  23.8 us
    another operation x1, other arithmetic, body(): jnp.stack([cos_rows * real_part - sin_rows * imag_part, cos_rows * imag_p...  20.3 us
    all_gather x1, waiting for transfers between devices, body(): every = lax.all_gather(column, 'blk', axis=0, tiled=True)  19.4 us
    another operation x1, other arithmetic  18.6 us
    convert_element_type x1, local copies, waits for them, and re-layouts, body(): turned = jnp.stack([cos_rows * real_part - sin_rows * imag_part, cos_rows...  14.5 us
    slice x1, local copies, waits for them, and re-layouts, body(): real_part, imag_part = (own[None, :, :, 0], own[None, :, :, 1])  10.3 us
    convert_element_type x1, local copies, waits for them, and re-layouts, body(): own = column.reshape(chans, seg_total, 2, BINS).astype(jnp.float32)  6.6 us
  transfers between devices with their start and end apart: 2, of which 2 were waited for; matrix products, arithmetic and copies ran while one was open for 37% of the time, Pallas kernels for 0%

commit v1 on v0

--- a/solution.py
+++ b/solution.py
@@ -4,11 +4,28 @@
 import numpy as np
 from jax import lax
 from jax.sharding import PartitionSpec as P
+from jax.lax import axis_index, axis_size, ppermute
 
 BINS = 128
 FIRST_BIN = 16
 SMOOTH = 64
 LAGS = 16
+
+
+def _show_racks(work_x, peer_axis):
+    value_now = axis_size(peer_axis)
+    answer, b_next, x_new = (value_now, axis_index(peer_axis), work_x.shape[0])
+    all_rows = []
+    for it in tuple(range(answer)):
+        all_rows.append((it, (it + 1) % answer))
+    state_next = jnp.zeros((*work_x.shape[:0], answer * x_new, *work_x.shape[1:]), work_x.dtype)
+    step_out = work_x
+    for i0 in [*range(answer)]:
+        left_arr = (b_next - i0) % answer
+        state_next = lax.dynamic_update_slice_in_dim(state_next, step_out, left_arr * x_new, axis=0)
+        if i0 < answer - 1:
+            step_out = ppermute(step_out, perm=all_rows, axis_name=peer_axis)
+    return state_next
 
 
 def dft_thirds(seglen):
@@ -78,7 +95,7 @@
     white = whiten(records.reshape(chans * segs, seglen), usable.reshape(chans * segs), fir_taps)
     slab = white.reshape(chans, segs * 2 * BINS)
     column = lax.all_gather(slab, "tm", axis=1, tiled=True)
-    every = lax.all_gather(column, "blk", axis=0, tiled=True)
+    every = _show_racks(column, "blk")
     lags_dev = LAGS // tm_count
     tables = lax.dynamic_slice_in_dim(
         jnp.asarray(lag_rows(seg_total, seglen)), tm_index * lags_dev, lags_dev, 1

time: 193 us -> 296 us (1.53)
  waiting for transfers between devices: 68 us -> 164 us
  local copies, waits for them, and re-layouts: 40.2 us -> 52.1 us
  matrix products: 28.6 us -> 23.9 us
    ppermute x0 -> x7, waiting for transfers between devices: none -> 115 us  [_show_racks(): step_out = ppermute(step_out, perm=all_rows, axis_name=peer_axis)]
    all_gather x1 -> x0, waiting for transfers between devices: 19.4 us -> none  [body(): every = lax.all_gather(column, 'blk', axis=0, tiled=True)]
    dynamic_update_slice x0 -> x8, local copies, waits for them, and re-layouts: none -> 8.8 us  [_show_racks(): lax.dynamic_update_slice_in_dim(state_next, step_out, left_arr * x_new, a...]
    dot_general x1, matrix products: 23.8 us -> 19 us  [body(): jnp.einsum('lik,jk->lij', left, every, preferred_element_type=jnp.float32)]
  transfers between devices with their start and end apart: 2 -> 8, of which waited for: 2 -> 7; matrix products, arithmetic and copies ran while one was open for 37% -> 27% of each run, Pallas kernels for 0% -> 0%
where the time goes in v1:
time: 296 us; the launch traced here: 295 us
  waiting for transfers between devices  164 us (55%)
  local copies, waits for them, and re-layouts  52.1 us (18%)
  other arithmetic  41.4 us (14%)
  matrix products  23.9 us (8%)
  between operations  13.6 us (5%)
    ppermute x7, waiting for transfers between devices, _show_racks(): step_out = ppermute(step_out, perm=all_rows, axis_name=peer_axis)  115 us
    all_gather x1, waiting for transfers between devices, body(): column = lax.all_gather(slab, 'tm', axis=1, tiled=True)  48.8 us
    another operation x1, other arithmetic, body(): jnp.stack([cos_rows * real_part - sin_rows * imag_part, cos_rows * imag_p...  20.2 us
    dot_general x1, matrix products, body(): jnp.einsum('lik,jk->lij', left, every, preferred_element_type=jnp.float32)  19 us
    another operation x1, other arithmetic  18.6 us
    convert_element_type x1, local copies, waits for them, and re-layouts, body(): turned = jnp.stack([cos_rows * real_part - sin_rows * imag_part, cos_rows...  14.4 us
    slice x1, local copies, waits for them, and re-layouts, body(): real_part, imag_part = (own[None, :, :, 0], own[None, :, :, 1])  9.11 us
    dynamic_update_slice x8, local copies, waits for them, and re-layouts, _show_racks(): lax.dynamic_update_slice_in_dim(state_next, step_out, left_arr * x_new, a...  8.8 us
  transfers between devices with their start and end apart: 8, of which 7 were waited for; matrix products, arithmetic and copies ran while one was open for 27% of the time, Pallas kernels for 0%

profile of v1, /device:TPU:0, one launch (start us, length us, event | category | flops | bytes accessed | tf_op | source)
XLA Modules:
  0.0 295.0 jit_solution(9926172988491476801)
XLA Ops:
  6.5 0.0 all-gather.2.cloned.1.call-start
  6.5 1.8 abs.10
  8.3 2.4 reshape.75
  10.7 0.7 dynamic-slice_convert_fusion
  11.4 0.1 copy.6
  11.6 0.1 convert_element_type.59
  11.7 0.7 rev.3
  12.5 0.1 pad.4
  12.5 0.2 broadcast_bitcast_fusion
  12.8 0.3 copy.8
  13.1 1.6 reshape.73
  14.7 1.1 abs.11
  15.8 1.7 fusion.11
  17.6 3.1 %multiply_reduce_fusion = (f32[1024]{0:T(1024)S(1)}, f32[1024,256]{0,1:T(8,128)S(1)}) fusion(f32[512,768]{1,0:T(8,128)S(1)} %fusion.11, f32[1024,512]{1,0:T(8,128)} %reshape.75, bf16[1024,512]{1,0:T(8,128)(2,1)} %abs.11, f32[512]{0:T(512)S(1)} %fusion.24), kind=kOutput, calls=%fused_computation.10 | convolution fusion | flops 809630720 | bytes 5773312 | tf_op jit(solution)/shard_map/dot_general | solution.py:83
  20.7 0.1 multiply_convert_fusion
  20.8 0.2 copy.7
  21.0 1.1 reshape.74
  22.1 0.0 all-gather.2.cloned.1.call-update
  22.1 48.8 %all-gather.2.cloned.1.call-done = bf16[256,4096]{1,0:T(8,128)(2,1)} async-done(((bf16[256,1024]{1,0:T(8,128)(2,1)}), bf16[256,4096]{1,0:T(8,128)(2,1)}) %all-gather.2.cloned.1.call-update) | async-done | bytes 2097168 | tf_op jit(solution)/shard_map/all_gather | solution.py:97
  70.9 0.0 collective-permute-start
  70.9 26.6 %collective-permute-done = bf16[256,4096]{1,0:T(8,128)(2,1)S(1)} collective-permute-done((bf16[256,4096]{1,0:T(8,128)(2,1)}, bf16[256,4096]{1,0:T(8,128)(2,1)S(1)}, u32[]{:S(2)}, u32[]{:S(2)}) %collective-permute-start) | collective-permute-done | bytes 2097184 | tf_op jit(solution)/shard_map/ppermute | solution.py:27
  97.5 0.0 copy-start.3
  97.5 0.0 collective-permute-start.1
  97.5 26.4 %collective-permute-done.1 = bf16[256,4096]{1,0:T(8,128)(2,1)S(1)} collective-permute-done((bf16[256,4096]{1,0:T(8,128)(2,1)S(1)}, bf16[256,4096]{1,0:T(8,128)(2,1)S(1)}, u32[]{:S(2)}, u32[]{:S(2)}) %collective-permute-start.1) | collective-permute-done | bytes 2097184 | tf_op jit(solution)/shard_map/ppermute | solution.py:27
  123.9 0.0 copy-start.1
  123.9 1.4 copy-done.1
  125.2 0.0 collective-permute-start.2
  125.2 26.5 %collective-permute-done.2 = bf16[256,4096]{1,0:T(8,128)(2,1)} collective-permute-done((bf16[256,4096]{1,0:T(8,128)(2,1)S(1)}, bf16[256,4096]{1,0:T(8,128)(2,1)}, u32[]{:S(2)}, u32[]{:S(2)}) %collective-permute-start.2) | collective-permute-done | bytes 2097184 | tf_op jit(solution)/shard_map/ppermute | solution.py:27
  151.7 0.0 copy-done.3
  151.7 0.0 collective-permute-start.3
  151.7 0.7 fusion.21
  152.4 6.6 %reshape.76 = f32[256,16,2,128]{3,2,1,0:T(2,128)} reshape(bf16[256,4096]{1,0:T(8,128)(2,1)} %all-gather.2.cloned.1.call-done) | data formatting | bytes 6291456 | tf_op jit(solution)/shard_map/convert_element_type | solution.py:105
  159.0 9.1 %fusion.33 = (f32[256,16,1,128]{3,2,1,0:T(1,128)S(1)}, f32[256,16,1,128]{3,2,1,0:T(1,128)}) fusion(f32[256,16,2,128]{3,2,1,0:T(2,128)} %reshape.76), kind=kLoop, calls=%fused_computation.48 | loop fusion | bytes 8388608 | tf_op jit(solution)/shard_map/slice | solution.py:106
  168.1 10.3 %collective-permute-done.3 = bf16[256,4096]{1,0:T(8,128)(2,1)} collective-permute-done((bf16[256,4096]{1,0:T(8,128)(2,1)}, bf16[256,4096]{1,0:T(8,128)(2,1)}, u32[]{:S(2)}, u32[]{:S(2)}) %collective-permute-start.3) | collective-permute-done | bytes 2097184 | tf_op jit(solution)/shard_map/ppermute | solution.py:27
  178.4 0.0 collective-permute-start.4
  178.4 18.6 %subtract_convert_fusion = (bf16[4,256,16,1,128]{4,3,2,1,0:T(2,128)(2,1)S(1)}, bf16[4,256,16,1,128]{4,3,2,1,0:T(2,128)(2,1)S(1)}) fusion(f32[256,16,128]{2,1,0:T(8,128)} %bitcast.29, f32[4,128]{1,0:T(4,128)S(1)} %get-tuple-element.10, f32[256,16,128]{2,1,0:T(8,128)S(1)} %bitcast.28, f32[4,128]{1,0:T(4,128)S(1)} %get-tuple-element.9), kind=kLoop, calls=%fused_computation.4 | loop fusion | flops 16777216 | bytes 12587008 | tf_op jit(solution)/shard_map/convert.2
  197.0 8.0 %collective-permute-done.4 = bf16[256,4096]{1,0:T(8,128)(2,1)} collective-permute-done((bf16[256,4096]{1,0:T(8,128)(2,1)}, bf16[256,4096]{1,0:T(8,128)(2,1)}, u32[]{:S(2)}, u32[]{:S(2)}) %collective-permute-start.4) | collective-permute-done | bytes 2097184 | tf_op jit(solution)/shard_map/ppermute | solution.py:27
  205.0 0.0 collective-permute-start.5
  205.0 20.2 %pad_maximum_fusion = bf16[4,256,16,2,128]{4,3,2,1,0:T(2,128)(2,1)} fusion(bf16[4,256,16,1,128]{4,3,2,1,0:T(2,128)(2,1)S(1)} %get-tuple-element.6, bf16[4,256,16,1,128]{4,3,2,1,0:T(2,128)(2,1)S(1)} %get-tuple-element.5), kind=kLoop, calls=%fused_computation.2 | loop fusion | flops 16777216 | bytes 16777216 | tf_op jit(solution)/shard_map/stack | solution.py:107
  225.2 14.4 %convert_element_type.63 = bf16[4,256,4096]{2,1,0:T(8,128)(2,1)} reshape(bf16[4,256,16,2,128]{4,3,2,1,0:T(2,128)(2,1)} %pad_maximum_fusion) | data formatting | bytes 16777216 | tf_op jit(solution)/shard_map/convert_element_type | solution.py:110
  239.7 0.0 copy-start
  239.7 0.0 copy-start.4
  239.7 1.9 broadcast_in_dim.15
  241.6 0.0 copy-done
  241.6 0.0 copy-start.2
  241.6 0.3 constant_dynamic-update-slice_fusion.7
  241.9 0.0 copy-done.4
  241.9 0.3 constant_dynamic-update-slice_fusion.6
  242.2 0.0 collective-permute-done.5
  242.2 0.1 collective-permute-start.6
  242.3 1.0 copy-done.2
  243.3 0.3 constant_dynamic-update-slice_fusion.5
  243.6 1.9 constant_dynamic-update-slice_fusion.4
  245.4 0.0 slice-start
  245.4 2.0 constant_dynamic-update-slice_fusion.3
  247.4 1.9 constant_dynamic-update-slice_fusion.2
  249.3 0.0 slice-start.1
  249.3 2.0 constant_dynamic-update-slice_fusion.1
  251.3 17.5 %collective-permute-done.6 = bf16[256,4096]{1,0:T(8,128)(2,1)S(1)} collective-permute-done((bf16[256,4096]{1,0:T(8,128)(2,1)}, bf16[256,4096]{1,0:T(8,128)(2,1)S(1)}, u32[]{:S(2)}, u32[]{:S(2)}) %collective-permute-start.6) | collective-permute-done | bytes 2097184 | tf_op jit(solution)/shard_map/ppermute | solution.py:27
  268.8 0.3 constant_dynamic-update-slice_fusion
  269.1 0.0 slice-done
  269.1 0.0 slice-done.1
  269.1 19.0 %fusion.2 = bf16[4,256,2048]{2,1,0:T(8,128)(2,1)} fusion(bf16[4,256,4096]{2,1,0:T(8,128)(2,1)S(1)} %bitcast.27, bf16[2048,4096]{1,0:T(8,128)(2,1)S(1)} %constant_dynamic-update-slice_fusion), kind=kOutput, calls=%fused_computation.5 | convolution fusion | flops 17181966336 | bytes 29360128 | tf_op jit(solution)/shard_map/lik,jk->lij/dot_general | solution.py:112
  (3 shorter events, 0.0 us)
Async XLA Ops:
  6.5 64.4 %all-gather.2.cloned.1.call-start = ((), (), s32[]{:S(2)}) async-start(), calls=%async_computation | async-start | bytes 2621440 | tf_op jit(solution)/shard_map/all_gather | solution.py:97
  70.9 26.6 %collective-permute-start = (bf16[256,4096]{1,0:T(8,128)(2,1)}, bf16[256,4096]{1,0:T(8,128)(2,1)S(1)}, u32[]{:S(2)}, u32[]{:S(2)}) collective-permute-start(bf16[256,4096]{1,0:T(8,128)(2,1)} %all-gather.2.cloned.1.call-done), channel_id=1, source_target_pairs={{0,4},{4,8},{8,12},{12,16},{16,20},{20,24},{24,28},{28,0},{1,5},{5... | collective-permute-start | bytes 6291464 | tf_op jit(solution)/shard_map/ppermute | solution.py:27
  97.5 54.2 %copy-start.3 = (bf16[256,4096]{1,0:T(8,128)(2,1)}, bf16[256,4096]{1,0:T(8,128)(2,1)S(1)}, u32[]{:S(2)}) copy-start(bf16[256,4096]{1,0:T(8,128)(2,1)S(1)} %collective-permute-done) | copy-start | bytes 6291460
  97.5 26.4 %collective-permute-start.1 = (bf16[256,4096]{1,0:T(8,128)(2,1)S(1)}, bf16[256,4096]{1,0:T(8,128)(2,1)S(1)}, u32[]{:S(2)}, u32[]{:S(2)}) collective-permute-start(bf16[256,4096]{1,0:T(8,128)(2,1)S(1)} %collective-permute-done), channel_id=1, source_target_pairs={{0,4},{4,8},{8,12},{12,16},{16,20},{20,24},{24,28},{28,0},{1,5},{5... | collective-permute-start | bytes 6291464 | tf_op jit(solution)/shard_map/ppermute | solution.py:27
  123.9 1.4 copy-start.1
  125.2 26.5 %collective-permute-start.2 = (bf16[256,4096]{1,0:T(8,128)(2,1)S(1)}, bf16[256,4096]{1,0:T(8,128)(2,1)}, u32[]{:S(2)}, u32[]{:S(2)}) collective-permute-start(bf16[256,4096]{1,0:T(8,128)(2,1)S(1)} %collective-permute-done.1), channel_id=1, source_target_pairs={{0,4},{4,8},{8,12},{12,16},{16,20},{20,24},{24,28},{28,0},{1,5},{5... | collective-permute-start | bytes 6291464 | tf_op jit(solution)/shard_map/ppermute | solution.py:27
  151.7 26.7 %collective-permute-start.3 = (bf16[256,4096]{1,0:T(8,128)(2,1)}, bf16[256,4096]{1,0:T(8,128)(2,1)}, u32[]{:S(2)}, u32[]{:S(2)}) collective-permute-start(bf16[256,4096]{1,0:T(8,128)(2,1)} %collective-permute-done.2), channel_id=1, source_target_pairs={{0,4},{4,8},{8,12},{12,16},{16,20},{20,24},{24,28},{28,0},{1,5},{5... | collective-permute-start | bytes 6291464 | tf_op jit(solution)/shard_map/ppermute | solution.py:27
  178.4 26.7 %collective-permute-start.4 = (bf16[256,4096]{1,0:T(8,128)(2,1)}, bf16[256,4096]{1,0:T(8,128)(2,1)}, u32[]{:S(2)}, u32[]{:S(2)}) collective-permute-start(bf16[256,4096]{1,0:T(8,128)(2,1)} %collective-permute-done.3), channel_id=1, source_target_pairs={{0,4},{4,8},{8,12},{12,16},{16,20},{20,24},{24,28},{28,0},{1,5},{5... | collective-permute-start | bytes 6291464 | tf_op jit(solution)/shard_map/ppermute | solution.py:27
  205.0 37.2 %collective-permute-start.5 = (bf16[256,4096]{1,0:T(8,128)(2,1)}, bf16[256,4096]{1,0:T(8,128)(2,1)}, u32[]{:S(2)}, u32[]{:S(2)}) collective-permute-start(bf16[256,4096]{1,0:T(8,128)(2,1)} %collective-permute-done.4), channel_id=1, source_target_pairs={{0,4},{4,8},{8,12},{12,16},{16,20},{20,24},{24,28},{28,0},{1,5},{5... | collective-permute-start | bytes 6291464 | tf_op jit(solution)/shard_map/ppermute | solution.py:27
  239.7 1.9 copy-start
  239.7 2.2 copy-start.4
  241.6 1.7 copy-start.2
  242.2 26.6 %collective-permute-start.6 = (bf16[256,4096]{1,0:T(8,128)(2,1)}, bf16[256,4096]{1,0:T(8,128)(2,1)S(1)}, u32[]{:S(2)}, u32[]{:S(2)}) collective-permute-start(bf16[256,4096]{1,0:T(8,128)(2,1)} %collective-permute-done.5), channel_id=1, source_target_pairs={{0,4},{4,8},{8,12},{12,16},{16,20},{20,24},{24,28},{28,0},{1,5},{5... | collective-permute-start | bytes 6291464 | tf_op jit(solution)/shard_map/ppermute | solution.py:27
  245.4 23.7 %slice-start = ((s8[8388608]{0:T(1024)(128)(4,1)}), s8[4194304]{0:T(1024)(128)(4,1)S(1)}, s32[]{:S(2)}) async-start(s8[8388608]{0:T(1024)(128)(4,1)} %bitcast.26), calls=%async_computation.1 | async-start | bytes 8388608
  249.3 19.8 %slice-start.1 = ((s8[8388608]{0:T(1024)(128)(4,1)}), s8[4194304]{0:T(1024)(128)(4,1)S(1)}, s32[]{:S(2)}) async-start(s8[8388608]{0:T(1024)(128)(4,1)} %bitcast.26), calls=%async_computation.2 | async-start | bytes 8388608
Sparse Core Ops, SparseCore 0:
  22.3 48.6 all-gather.1
